TPU v7x, 32 devices: a whole 2x2x4 slice. The times are simulated.
32 devices in a mesh: ingest: 4 (over x, core), pair: 8 (over z, y).
Axes of the slice: x: 2, y: 2, z: 4, core: 2. Of those that a mesh axis runs over, the one named last changes fastest.
Arguments:
- embeddings: bfloat16 [12288, 768], P(('ingest', 'pair')), may hold values from -8 to 8
- centroids: bfloat16 [16, 768], replicated, may hold values from -6 to 6
- cluster: int32 [12288], P(('ingest', 'pair')), may hold values from 0 to 15, as said below
- labels: int32 [12288], P(('ingest', 'pair')), may hold values from 0 to 127
Outputs:
- weight: float32 [12288], P(('ingest', 'pair'))
- label_sums: float32 [12288, 128], P(('ingest', 'pair'))
Inputs may be any that keep to these rules, and one draw needn't show every extreme that they name: Among the rows of one device, at most 192 name clusters of the same ingest index (the same cluster // 4). Among the rows of one device, at most 96 name the same cluster.
All inputs are finite; a program needn't handle non-finite values.
Results may differ from a plain program's by a relative error of at most 0.0014.
Values may be sent and summed in bfloat16 or wider, within the bound.
A program may use at most 64 MiB of HBM per device.

v0:
```python
import math

import jax
import jax.numpy as jnp
from jax import lax
from jax.sharding import PartitionSpec as P

LABELS = 128


SHARPNESS = 8.0
EPSILON = 1e-06


def swapped(value, axis, distance):
    return lax.ppermute(value, axis, [(i, i ^ 1 << distance) for i in range(lax.axis_size(axis))])


def unit_rows(embeddings, centroids, cluster):
    lookup = (cluster[:, None] == jnp.arange(centroids.shape[0], dtype=jnp.int32)[None, :]).astype(
        jnp.bfloat16
    )
    centre = jnp.dot(lookup, centroids, preferred_element_type=jnp.float32)
    shifted = centre + embeddings.astype(jnp.float32)
    scale_row = lax.rsqrt(jnp.sum(shifted * shifted, axis=1, keepdims=True) + EPSILON)
    return (shifted * scale_row).astype(jnp.bfloat16)


def kernel_block(queries, query_cluster, key_rows, key_cluster):
    scores = lax.dot_general(
        queries, key_rows, (((1,), (1,)), ((), ())), preferred_element_type=jnp.float32
    )
    same_cluster = (query_cluster[:, None] == key_cluster[None, :]) & (query_cluster[:, None] >= 0)
    return jnp.where(same_cluster, jnp.exp(SHARPNESS * (scores - 1.0)), 0.0)


def label_table(label_ids):
    return (label_ids[:, None] == jnp.arange(LABELS, dtype=jnp.int32)[None, :]).astype(jnp.bfloat16)


def row_terms(kernel, rounded, table):
    return (jnp.sum(kernel, axis=1), jnp.dot(rounded, table, preferred_element_type=jnp.float32))


def rank_among(target, count):
    hits = (target[:, None] == jnp.arange(count, dtype=jnp.int32)[None, :]).astype(jnp.int32)
    return jnp.sum((jnp.cumsum(hits, axis=0) - 1) * hits, axis=1)


def pack_rows(unit, cluster, labels, slot_index, total_slots):
    send_rows = jnp.zeros((total_slots, unit.shape[1]), jnp.bfloat16).at[slot_index].set(unit)
    send_meta = (
        jnp.full((total_slots, 2), -1, jnp.int32)
        .at[slot_index]
        .set(jnp.stack([cluster, labels], axis=1))
    )
    return (send_rows, send_meta)


def cluster_terms(queries, query_meta, key_sets):
    slot_count, width = queries.shape
    block_rows = math.gcd(slot_count, 512)
    tables = [label_table(key_set[1][:, 1]) for key_set in key_sets]

    def one_block(parts):
        block_queries, block_meta = parts
        density = jnp.zeros((block_rows,), jnp.float32)
        label_sum = jnp.zeros((block_rows, LABELS), jnp.float32)
        for key_set, table in zip(key_sets, tables):
            kernel = kernel_block(block_queries, block_meta[:, 0], key_set[0], key_set[1][:, 0])
            density_part, label_part = row_terms(kernel, kernel.astype(jnp.bfloat16), table)
            density = density + density_part
            label_sum = label_sum + label_part
        return (density, label_sum)

    stacked = (
        queries.reshape(slot_count // block_rows, block_rows, width),
        query_meta.reshape(slot_count // block_rows, block_rows, 2),
    )
    density, label_sum = lax.map(one_block, stacked)
    return (density.reshape(slot_count), label_sum.reshape(slot_count, LABELS))


def on_device(embeddings, centroids, cluster, labels):
    rows_here = embeddings.shape[0]
    ingest_count = lax.axis_size("ingest")
    cluster_count = centroids.shape[0]
    group_clusters = cluster_count // ingest_count
    unit = unit_rows(embeddings, centroids, cluster)
    pair_count = lax.axis_size("pair")
    half_cap = max(1, 2 * rows_here // cluster_count)
    rank = rank_among(cluster, cluster_count)
    home = cluster // group_clusters * pair_count + 2 * (cluster % group_clusters) + rank % 2
    slot_index = home * half_cap + rank // 2
    send_rows, send_meta = pack_rows(
        unit, cluster, labels, slot_index, ingest_count * pair_count * half_cap
    )
    queries, query_meta = (
        lax.all_to_all(send_rows, ("ingest", "pair"), split_axis=0, concat_axis=0, tiled=True),
        lax.all_to_all(send_meta, ("ingest", "pair"), split_axis=0, concat_axis=0, tiled=True),
    )
    partner_rows, partner_meta = swapped((queries, query_meta), "pair", 0)
    density, label_sum = cluster_terms(
        queries, query_meta, ((queries, query_meta), (partner_rows, partner_meta))
    )
    home_density, home_labels = (
        lax.all_to_all(density, ("ingest", "pair"), split_axis=0, concat_axis=0, tiled=True),
        lax.all_to_all(label_sum, ("ingest", "pair"), split_axis=0, concat_axis=0, tiled=True),
    )
    return (1.0 / home_density[slot_index], home_labels[slot_index])


def solution(mesh):
    in_specs = (P(("ingest", "pair"), None), P(), P(("ingest", "pair")), P(("ingest", "pair")))
    out_specs = (P(("ingest", "pair")), P(("ingest", "pair"), None))
    return jax.shard_map(
        on_device, mesh=mesh, in_specs=in_specs, out_specs=out_specs, check_vma=False
    )
```

profile of v0, /device:TPU:0, one launch (start us, length us, event | category | flops | bytes accessed | tf_op | source)
XLA Modules:
  0.0 195.6 jit_solution(18065277749526532329)
XLA Ops:
  0.6 0.0 copy-start
  0.6 0.7 fusion.42
  1.3 0.9 reduce-window.6
  2.2 0.2 slice_reduce_fusion.2
  2.4 0.8 fusion.41
  3.2 0.7 compare_select_fusion
  3.9 0.0 copy-done
  3.9 2.5 %multiply_reduce_fusion = (f32[384]{0:T(512)S(1)}, f32[384,768]{1,0:T(8,128)}) fusion(bf16[384,768]{1,0:T(8,128)(2,1)} %param.6, bf16[16,768]{1,0:T(8,128)(2,1)S(1)} %copy-done, s32[384]{0:T(512)} %param.8), kind=kOutput, calls=%fused_computation.40 | convolution fusion | flops 10622592 | bytes 1797120 | tf_op jit(solution)/shard_map/dot_general | solution.py:23
  6.4 3.6 %scatter_custom_fusion.1 = bf16[1536,768]{1,0:T(8,128)(2,1)S(1)} fusion(s32[384]{0:T(512)S(1)} %compare_select_fusion, bf16[]{:T(256)} %constant.105.clone.1, f32[384,768]{1,0:T(8,128)} %get-tuple-element.270, f32[384]{0:T(512)S(1)} %add_rsqrt_fusion), kind=kCustom, calls=%fused_computation.41 | custom fusion | flops 589824 | bytes 3540994 | tf_op jit(solution)/shard_map/scatter | solution.py:51
  10.1 0.0 copy-start.1
  10.1 0.0 copy-start.2
  10.1 62.9 %all_to_all.48 = bf16[32,48,768]{2,1,0:T(8,128)(2,1)} all-to-all(bf16[32,48,768]{2,1,0:T(8,128)(2,1)S(1)} %bitcast.71), channel_id=1, replica_groups=mesh['ingest'=4,'pair'=8] {'ingest','pair'}, dimensions={0} | all-to-all | bytes 4718592 | tf_op jit(solution)/shard_map/all_to_all | solution.py:99
  73.0 0.9 collective-permute-start.1
  73.9 0.0 copy-done.1
  73.9 0.0 copy-done.2
  73.9 0.1 copy.19
  74.1 1.6 scatter_custom_fusion
  75.7 0.9 copy.20
  76.6 2.8 %all-to-all-start = ((s32[32,48,2]{1,2,0:T(2,128)}), s32[32,48,2]{1,2,0:T(2,128)S(1)}, u32[]{:S(2)}, u32[]{:S(2)}) async-start(s32[32,48,2]{1,2,0:T(2,128)} %copy.20), calls=%async_computation | async-start | bytes 65536 | tf_op jit(solution)/shard_map/all_to_all | solution.py:100
  79.5 47.0 %all-to-all-done = s32[32,48,2]{1,2,0:T(2,128)S(1)} async-done(((s32[32,48,2]{1,2,0:T(2,128)}), s32[32,48,2]{1,2,0:T(2,128)S(1)}, u32[]{:S(2)}, u32[]{:S(2)}) %all-to-all-start) | async-done | bytes 12320 | tf_op jit(solution)/shard_map/all_to_all | solution.py:100
  126.4 0.1 all_to_all.34
  126.5 1.4 collective-permute-start
  128.0 0.1 reshape.71
  128.1 2.2 %collective-permute-done = s32[1536,2]{0,1:T(2,128)S(1)} collective-permute-done((s32[1536,2]{0,1:T(2,128)S(1)}, s32[1536,2]{0,1:T(2,128)S(1)}, u32[]{:S(2)}, u32[]{:S(2)}) %collective-permute-start) | collective-permute-done | bytes 12320 | tf_op jit(solution)/shard_map/ppermute | solution.py:16
  130.3 0.0 collective-permute-done.1
  130.3 29.3 %while.16 = (s32[]{:T(128)}, f32[3,512]{1,0:T(4,128)S(1)}, f32[3,512,128]{2,1,0:T(8,128)}, s32[3,512,2]{1,0,2:T(4,128)S(1)}, s32[1536,2]{0,1:T(2,128)S(1)}, /*in...) while((s32[]{:T(128)}, f32[3,512]{1,0:T(4,128)S(1)}, ...), condition=%wide.region_9.10_spmd.clone, body=%wide.region_6.9_spmd.clone.sunk | while | flops 2830434304 | bytes 13462661 | solution.py:80
  130.5 3.8 %fusion.78 = (f32[512]{0:T(512)S(1)}, bf16[512,1536]{1,0:T(8,128)(2,1)S(1)}) fusion(bf16[1536,768]{1,0:T(8,128)(2,1)} %get-tuple-element.388, bf16[3,512,768]{2,1,0:T(8,128)(2,1)} %get-tuple-element.385, s32[]{:T(128)} %get-tuple-element.367, pred[512]{0:T(512)(128)(4,1)S(1)} %compare_reduce_fusion.2, s32[1536]{0:T(1024)S(1)} %get-tuple-element.350, ...), kind=kOutput, calls=%fused_computation.85.clone.1 | convolution fusion | flops 1213464064 | bytes 4729856 | tf_op jit(solution)/shard_map/while/body/eval_jaxpr/dot_general | solution.py:30
  134.2 0.7 fusion.79
  134.9 3.8 %fusion.77 = (f32[512]{0:T(512)S(1)}, bf16[512,1536]{1,0:T(8,128)(2,1)S(1)}) fusion(bf16[1536,768]{1,0:T(8,128)(2,1)} %get-tuple-element.386, bf16[3,512,768]{2,1,0:T(8,128)(2,1)} %get-tuple-element.385, s32[]{:T(128)} %get-tuple-element.367, pred[512]{0:T(512)(128)(4,1)S(1)} %compare_reduce_fusion.2, s32[1536]{0:T(1024)S(1)} %get-tuple-element.348, ...), kind=kOutput, calls=%fused_computation.84.clone.1 | convolution fusion | flops 1213464064 | bytes 4729856 | tf_op jit(solution)/shard_map/while/body/eval_jaxpr/dot_general | solution.py:30
  138.7 1.4 fusion.80
  140.2 3.8 %fusion.78 = (f32[512]{0:T(512)S(1)}, bf16[512,1536]{1,0:T(8,128)(2,1)S(1)}) fusion(bf16[1536,768]{1,0:T(8,128)(2,1)} %get-tuple-element.388, bf16[3,512,768]{2,1,0:T(8,128)(2,1)} %get-tuple-element.385, s32[]{:T(128)} %get-tuple-element.367, pred[512]{0:T(512)(128)(4,1)S(1)} %compare_reduce_fusion.2, s32[1536]{0:T(1024)S(1)} %get-tuple-element.350, ...), kind=kOutput, calls=%fused_computation.85.clone.1 | convolution fusion | flops 1213464064 | bytes 4729856 | tf_op jit(solution)/shard_map/while/body/eval_jaxpr/dot_general | solution.py:30
  144.0 0.7 fusion.79
  144.7 3.8 %fusion.77 = (f32[512]{0:T(512)S(1)}, bf16[512,1536]{1,0:T(8,128)(2,1)S(1)}) fusion(bf16[1536,768]{1,0:T(8,128)(2,1)} %get-tuple-element.386, bf16[3,512,768]{2,1,0:T(8,128)(2,1)} %get-tuple-element.385, s32[]{:T(128)} %get-tuple-element.367, pred[512]{0:T(512)(128)(4,1)S(1)} %compare_reduce_fusion.2, s32[1536]{0:T(1024)S(1)} %get-tuple-element.348, ...), kind=kOutput, calls=%fused_computation.84.clone.1 | convolution fusion | flops 1213464064 | bytes 4729856 | tf_op jit(solution)/shard_map/while/body/eval_jaxpr/dot_general | solution.py:30
  148.4 1.4 fusion.80
  150.0 3.8 %fusion.78 = (f32[512]{0:T(512)S(1)}, bf16[512,1536]{1,0:T(8,128)(2,1)S(1)}) fusion(bf16[1536,768]{1,0:T(8,128)(2,1)} %get-tuple-element.388, bf16[3,512,768]{2,1,0:T(8,128)(2,1)} %get-tuple-element.385, s32[]{:T(128)} %get-tuple-element.367, pred[512]{0:T(512)(128)(4,1)S(1)} %compare_reduce_fusion.2, s32[1536]{0:T(1024)S(1)} %get-tuple-element.350, ...), kind=kOutput, calls=%fused_computation.85.clone.1 | convolution fusion | flops 1213464064 | bytes 4729856 | tf_op jit(solution)/shard_map/while/body/eval_jaxpr/dot_general | solution.py:30
  153.8 0.7 fusion.79
  154.5 3.8 %fusion.77 = (f32[512]{0:T(512)S(1)}, bf16[512,1536]{1,0:T(8,128)(2,1)S(1)}) fusion(bf16[1536,768]{1,0:T(8,128)(2,1)} %get-tuple-element.386, bf16[3,512,768]{2,1,0:T(8,128)(2,1)} %get-tuple-element.385, s32[]{:T(128)} %get-tuple-element.367, pred[512]{0:T(512)(128)(4,1)S(1)} %compare_reduce_fusion.2, s32[1536]{0:T(1024)S(1)} %get-tuple-element.348, ...), kind=kOutput, calls=%fused_computation.84.clone.1 | convolution fusion | flops 1213464064 | bytes 4729856 | tf_op jit(solution)/shard_map/while/body/eval_jaxpr/dot_general | solution.py:30
  158.2 1.4 fusion.80
  159.7 0.1 all_to_all.38
  159.8 9.6 %all_to_all.49 = f32[32,48,1]{1,2,0:T(1,128)S(1)} all-to-all(f32[32,48,1]{1,2,0:T(1,128)S(1)} %all_to_all.38), channel_id=1, replica_groups=mesh['ingest'=4,'pair'=8] {'ingest','pair'}, dimensions={0} | all-to-all | bytes 12288 | tf_op jit(solution)/shard_map/all_to_all | solution.py:107
  169.4 2.6 %all-to-all-start.3 = ((f32[32,48,128]{2,1,0:T(8,128)}), f32[32,48,128]{2,1,0:T(8,128)S(1)}, u32[]{:S(2)}, u32[]{:S(2)}) async-start(f32[32,48,128]{2,1,0:T(8,128)} %bitcast.6), calls=%async_computation.3 | async-start | bytes 1572864 | tf_op jit(solution)/shard_map/all_to_all | solution.py:108
  172.0 0.5 broadcast.113
  172.5 0.7 reduce.15
  173.2 0.1 all_to_all.40
  173.3 2.5 %gather_fusion = f32[384]{0:T(512)S(1)} fusion(f32[1536]{0:T(1024)S(1)} %all_to_all.40, s32[1024]{0:T(1024)S(1)} %pad_clamp_fusion), kind=kCustom, calls=%fused_computation | custom fusion | bytes 4608 | tf_op jit(solution)/shard_map/gather | solution.py:110
  175.8 0.6 broadcast_divide_fusion
  176.4 17.6 %all-to-all-done.3 = f32[32,48,128]{2,1,0:T(8,128)S(1)} async-done(((f32[32,48,128]{2,1,0:T(8,128)}), f32[32,48,128]{2,1,0:T(8,128)S(1)}, u32[]{:S(2)}, u32[]{:S(2)}) %all-to-all-start.3) | async-done | bytes 786464 | tf_op jit(solution)/shard_map/all_to_all | solution.py:108
  194.0 1.6 gather_fusion.1
  (32 shorter events, 0.4 us)
Async XLA Ops:
  0.6 3.3 %copy-start = (bf16[16,768]{1,0:T(8,128)(2,1)S(1)}, bf16[16,768]{1,0:T(8,128)(2,1)}, u32[]{:S(2)}) copy-start(bf16[16,768]{1,0:T(8,128)(2,1)} %param.7) | copy-start | bytes 73732
  10.1 63.8 %copy-start.1 = (s32[384]{0:T(512)S(1)}, s32[384]{0:T(512)}, u32[]{:S(2)}) copy-start(s32[384]{0:T(512)} %param.8) | copy-start | bytes 4612
  10.1 63.8 %copy-start.2 = (s32[384]{0:T(512)S(1)}, s32[384]{0:T(512)}, u32[]{:S(2)}) copy-start(s32[384]{0:T(512)} %param.9) | copy-start | bytes 4612
  73.0 57.4 %collective-permute-start.1 = (bf16[1536,768]{1,0:T(8,128)(2,1)}, bf16[1536,768]{1,0:T(8,128)(2,1)}, u32[]{:S(2)}, u32[]{:S(2)}) collective-permute-start(bf16[1536,768]{1,0:T(8,128)(2,1)} %bitcast.5), channel_id=1, source_target_pairs={{0,1},{1,0},{2,3},{3,2},{4,5},{5,4},{6,7},{7,6},{8,9},{9,8},{10,11... | collective-permute-start | bytes 7077896 | tf_op jit(solution)/shard_map/ppermute | solution.py:16
  76.6 49.8 %all-to-all-start = ((s32[32,48,2]{1,2,0:T(2,128)}), s32[32,48,2]{1,2,0:T(2,128)S(1)}, u32[]{:S(2)}, u32[]{:S(2)}) async-start(s32[32,48,2]{1,2,0:T(2,128)} %copy.20), calls=%async_computation | async-start | bytes 65536 | tf_op jit(solution)/shard_map/all_to_all | solution.py:100
  126.5 3.8 %collective-permute-start = (s32[1536,2]{0,1:T(2,128)S(1)}, s32[1536,2]{0,1:T(2,128)S(1)}, u32[]{:S(2)}, u32[]{:S(2)}) collective-permute-start(s32[1536,2]{0,1:T(2,128)S(1)} %all_to_all.34), channel_id=1, source_target_pairs={{0,1},{1,0},{2,3},{3,2},{4,5},{5,4},{6,7},{7,6},{8,9},{9,8},{10,11... | collective-permute-start | bytes 36872 | tf_op jit(solution)/shard_map/ppermute | solution.py:16
  169.4 24.6 %all-to-all-start.3 = ((f32[32,48,128]{2,1,0:T(8,128)}), f32[32,48,128]{2,1,0:T(8,128)S(1)}, u32[]{:S(2)}, u32[]{:S(2)}) async-start(f32[32,48,128]{2,1,0:T(8,128)} %bitcast.6), calls=%async_computation.3 | async-start | bytes 1572864 | tf_op jit(solution)/shard_map/all_to_all | solution.py:108
where the time goes:
time: 196 us
  blocking collectives  72.5 us (37%)
  waiting for transfers between devices  66.8 us (34%)
  matrix products  31.3 us (16%)
  local copies, waits for them, and re-layouts  8.23 us (4%)
  other arithmetic  8.08 us (4%)
  starting transfers between devices  7.78 us (4%)
    all_to_all x1, blocking collectives, on_device(): lax.all_to_all(send_rows, ('ingest', 'pair'), split_axis=0, concat_axis=0...  62.9 us
    all_to_all x1, waiting for transfers between devices, on_device(): lax.all_to_all(send_meta, ('ingest', 'pair'), split_axis=0, concat_axis=0...  47 us
    dot_general x6, matrix products, kernel_block(): lax.dot_general(queries, key_rows, (((1,), (1,)), ((), ())), preferred_el...  22.6 us
    all_to_all x1, waiting for transfers between devices, on_device(): lax.all_to_all(label_sum, ('ingest', 'pair'), split_axis=0, concat_axis=0...  17.6 us
    all_to_all x1, blocking collectives, on_device(): lax.all_to_all(density, ('ingest', 'pair'), split_axis=0, concat_axis=0,...  9.58 us
    dot_general x6, matrix products, row_terms(): jnp.dot(rounded, table, preferred_element_type=jnp.float32)  6.3 us
    gather x2, local copies, waits for them, and re-layouts, on_device(): return (1.0 / home_density[slot_index], home_labels[slot_index])  4.15 us
  transfers between devices with their start and end apart: 4, of which 3 were waited for; matrix products, arithmetic and copies ran while one was open for 4% of the time, Pallas kernels for 0%

commit v1 on v0

v1 whole, which is shorter than its diff:
```python
import functools

import jax
import jax.numpy as jnp
from jax import lax
from jax.experimental import pallas as pl
from jax.experimental.pallas import tpu as pltpu
from jax.sharding import PartitionSpec as P

LABELS = 128
SHARPNESS = 8.0
EPSILON = 1e-06
CORES = 2
MESH = pl.DeviceIdType.MESH


class Plan:
    def __init__(self, mesh_shape, rows, width, clusters):
        self.groups = mesh_shape["ingest"]
        self.sub = mesh_shape["pair"] // self.groups
        self.xs = mesh_shape["ingest"] // CORES
        self.rows = rows
        self.width = width
        self.clusters = clusters
        self.group_clusters = clusters // self.groups
        self.cap = 2 * rows // self.groups
        self.slots = self.groups * self.cap
        self.places = self.xs * self.sub * CORES
        self.chunk = 256 if self.slots % 256 == 0 else 128

    def place(self, dx, dy, dc):
        return (dx % self.xs * self.sub + dy % self.sub) * CORES + dc % CORES

    def offsets(self):
        return [
            (dx, dy, dc)
            for dx in range(self.xs)
            for dy in range(self.sub)
            for dc in range(CORES)
            if dx or dy or dc
        ]


def group_of(plan, cluster):
    group = jnp.zeros(cluster.shape, jnp.int32)
    for g in range(1, plan.groups):
        group = group + (cluster >= g * plan.group_clusters).astype(jnp.int32)
    return group


def column_of(row):
    parts = []
    eye = lax.broadcasted_iota(jnp.int32, (128, 128), 0) == lax.broadcasted_iota(
        jnp.int32, (128, 128), 1
    )
    for b in range(row.shape[1] // 128):
        parts.append(
            jnp.sum(jnp.where(eye, row[:, b * 128 : (b + 1) * 128], 0), axis=1, keepdims=True)
        )
    return jnp.concatenate(parts, axis=0)


def row_of(column):
    parts = []
    eye = lax.broadcasted_iota(jnp.int32, (128, 128), 0) == lax.broadcasted_iota(
        jnp.int32, (128, 128), 1
    )
    for b in range(column.shape[0] // 128):
        parts.append(
            jnp.sum(jnp.where(eye, column[b * 128 : (b + 1) * 128, :], 0), axis=0, keepdims=True)
        )
    return jnp.concatenate(parts, axis=1)


def kernel(
    plan,
    emb_ref,
    cent_ref,
    ccol_ref,
    crow_ref,
    lcol_ref,
    weight_ref,
    label_ref,
    packed,
    keys,
    codes,
    code_tx,
    code_rx,
    qcol,
    poscol,
    dens_acc,
    lab_acc,
    dens_tx,
    dens_rx,
    lab_rx,
    send_sem,
    row_sem,
    code_rx_sem,
    code_sem,
    dens_sem,
    lab_sem,
):
    G, cap, slots, sub = plan.groups, plan.cap, plan.slots, plan.sub
    ingest = lax.axis_index("ingest")
    pair = lax.axis_index("pair")
    x, core = ingest // CORES, ingest % CORES
    z, y = pair // sub, pair % sub

    def plane_device(dx, dy, dc):
        return (
            lax.rem(x + dx, plan.xs) * CORES + lax.rem(core + dc, CORES),
            z * sub + lax.rem(y + dy, sub),
        )

    def column_device(dz):
        return (ingest, lax.rem(z + dz, G) * sub + y)

    barrier = pltpu.get_barrier_semaphore()
    for dz in range(1, G):
        pl.semaphore_signal(barrier, inc=1, device_id=column_device(dz), device_id_type=MESH)
    for offset in plan.offsets():
        pl.semaphore_signal(barrier, inc=1, device_id=plane_device(*offset), device_id_type=MESH)

    def slot_of(cluster, rank):
        block = z - group_of(plan, cluster)
        block = jnp.where(block < 0, block + G, block)
        return block * cap + rank

    rows = plan.rows
    ccol, crow = ccol_ref[...], crow_ref[...]
    same = group_of(plan, ccol) == group_of(plan, crow)
    first = lax.broadcasted_iota(jnp.int32, (rows, rows), 0)
    second = lax.broadcasted_iota(jnp.int32, (rows, rows), 1)
    rank_row = jnp.sum(jnp.where(same & (first < second), 1, 0), axis=0, keepdims=True)
    rank_col = jnp.sum(jnp.where(same & (second < first), 1, 0), axis=1, keepdims=True)
    pos_row = slot_of(crow, rank_row)
    pos_col = slot_of(ccol, rank_col)
    poscol[...] = pos_col
    code_col = ccol * LABELS + lcol_ref[...] + 1
    lane = lax.broadcasted_iota(jnp.int32, (rows, slots), 1)
    code_tx[...] = jnp.sum(jnp.where(pos_col == lane, code_col, 0), axis=0, keepdims=True)

    lookup = (ccol == lax.broadcasted_iota(jnp.int32, (rows, plan.clusters), 1)).astype(
        jnp.float32
    ).astype(jnp.bfloat16)
    centre = jnp.dot(lookup, cent_ref[...], preferred_element_type=jnp.float32)
    shifted = centre + emb_ref[...].astype(jnp.float32)
    scale = lax.rsqrt(jnp.sum(shifted * shifted, axis=1, keepdims=True) + EPSILON)
    unit = (shifted * scale).astype(jnp.bfloat16)
    for b in range(G):
        pick = (
            lax.broadcasted_iota(jnp.int32, (cap, rows), 0) + b * cap == pos_row
        ).astype(jnp.float32).astype(jnp.bfloat16)
        block = jnp.dot(pick, unit, preferred_element_type=jnp.float32).astype(jnp.bfloat16)
        if b == 0:
            keys[0, pl.ds(0, cap), :] = block
        else:
            packed[pl.ds(b * cap, cap), :] = block

    pl.semaphore_wait(barrier, G - 1 + plan.places - 1)

    sent = []

    def send(src, dst, sem, device):
        copy = pltpu.make_async_remote_copy(
            src_ref=src,
            dst_ref=dst,
            send_sem=send_sem.at[len(sent)],
            recv_sem=sem,
            device_id=device,
            device_id_type=MESH,
        )
        copy.start()
        sent.append(copy)

    def arrive(dst, sem):
        pltpu.make_async_remote_copy(
            src_ref=dst,
            dst_ref=dst,
            send_sem=send_sem.at[0],
            recv_sem=sem,
            device_id=column_device(1),
            device_id_type=MESH,
        ).wait_recv()

    def part(place, b):
        return keys.at[place, pl.ds(b * cap, cap)]

    def pass_on(src_place, to_place, b, device):
        send(part(src_place, b), part(to_place, b), row_sem.at[to_place, b], device)

    def rows_arrive(place, b):
        arrive(part(place, b), row_sem.at[place, b])

    xrange, yrange = range(1, plan.xs), range(1, sub)

    def spread(b):
        for dx in xrange:
            pass_on(0, plan.place(-dx, 0, 0), b, plane_device(dx, 0, 0))
        for dy in yrange:
            pass_on(0, plan.place(0, -dy, 0), b, plane_device(0, dy, 0))
        pass_on(0, plan.place(0, 0, 1), b, plane_device(0, 0, 1))

    def forward_near(b):
        for dx in xrange:
            rows_arrive(plan.place(dx, 0, 0), b)
            if b % 2 == 0:
                for dy in yrange:
                    pass_on(
                        plan.place(dx, 0, 0), plan.place(dx, -dy, 0), b, plane_device(0, dy, 0)
                    )
            pass_on(plan.place(dx, 0, 0), plan.place(dx, 0, 1), b, plane_device(0, 0, 1))
        for dy in yrange:
            rows_arrive(plan.place(0, dy, 0), b)
            if b % 2 == 1:
                for dx in xrange:
                    pass_on(
                        plan.place(0, dy, 0), plan.place(-dx, dy, 0), b, plane_device(dx, 0, 0)
                    )
            pass_on(plan.place(0, dy, 0), plan.place(0, dy, 1), b, plane_device(0, 0, 1))

    def forward_far(b):
        for dx in xrange:
            for dy in yrange:
                rows_arrive(plan.place(dx, dy, 0), b)
                pass_on(plan.place(dx, dy, 0), plan.place(dx, dy, 1), b, plane_device(0, 0, 1))

    for b in range(1, G):
        send(code_tx, code_rx.at[b], code_rx_sem.at[b], column_device(G - b))
    for b in range(1, G):
        send(
            packed.at[pl.ds(b * cap, cap)], part(0, b), row_sem.at[0, b], column_device(G - b)
        )
    spread(0)

    lane_row = lax.broadcasted_iota(jnp.int32, (1, slots), 1)

    def block_lanes(b):
        return (lane_row >= b * cap) & (lane_row < (b + 1) * cap)

    code = jnp.where(block_lanes(0), code_tx[...], 0)
    for b in range(1, G):
        arrive(code_rx.at[b], code_rx_sem.at[b])
        code = code + jnp.where(block_lanes(b), code_rx[b], 0)
    codes[0] = code
    for offset in plan.offsets():
        to = plan.place(*(-step for step in offset))
        send(codes.at[0], codes.at[to], code_sem.at[to], plane_device(*offset))
    qcol[...] = (column_of(code) - 1) >> 7
    dens_acc[...] = jnp.zeros_like(dens_acc)
    lab_acc[...] = jnp.zeros_like(lab_acc)
    for offset in plan.offsets():
        arrive(codes.at[plan.place(*offset)], code_sem.at[plan.place(*offset)])

    chunk = plan.chunk
    steps = slots // chunk

    def compute(place):
        def body(step, carry):
            start = pl.multiple_of(step * chunk, chunk)
            key_rows = keys[place, pl.ds(start, chunk), :]
            key_code = codes[place, :, pl.ds(start, chunk)] - 1
            scores = lax.dot_general(
                keys[0], key_rows, (((1,), (1,)), ((), ())), preferred_element_type=jnp.float32
            )
            value = jnp.where(
                qcol[...] == key_code >> 7,
                jnp.exp(SHARPNESS * scores - SHARPNESS),
                0.0,
            )
            part_sum = value[:, :128]
            for b in range(1, chunk // 128):
                part_sum = part_sum + value[:, b * 128 : (b + 1) * 128]
            dens_acc[...] += part_sum
            table = (
                lax.broadcasted_iota(jnp.int32, (LABELS, chunk), 0) == (key_code & (LABELS - 1))
            ).astype(jnp.float32).astype(jnp.bfloat16)
            lab_acc[...] += lax.dot_general(
                value.astype(jnp.bfloat16),
                table,
                (((1,), (1,)), ((), ())),
                preferred_element_type=jnp.float32,
            )
            return carry

        lax.fori_loop(0, steps, body, 0)

    for b in range(1, G):
        rows_arrive(0, b)
        spread(b)
        forward_near(b - 1)
        if b >= 2:
            forward_far(b - 2)

    def arrived(place):
        for b in range(G):
            rows_arrive(place, b)

    forward_far(G - 2)
    compute(0)
    forward_near(G - 1)
    arrived(plan.place(0, 0, 1))
    compute(plan.place(0, 0, 1))
    near = [(dx, 0) for dx in xrange] + [(0, dy) for dy in yrange]
    for dx, dy in near:
        compute(plan.place(dx, dy, 0))
    forward_far(G - 1)
    for dx, dy in near:
        arrived(plan.place(dx, dy, 1))
        compute(plan.place(dx, dy, 1))
    for dx in xrange:
        for dy in yrange:
            compute(plan.place(dx, dy, 0))
            arrived(plan.place(dx, dy, 1))
            compute(plan.place(dx, dy, 1))

    for b in range(1, G):
        send(
            lab_acc.at[pl.ds(b * cap, cap)],
            lab_rx.at[pl.ds(b * cap, cap)],
            lab_sem.at[b],
            column_device(b),
        )
    dens_row = row_of(jnp.sum(dens_acc[...], axis=1, keepdims=True))
    dens_tx[...] = dens_row
    for b in range(1, G):
        send(dens_tx, dens_rx.at[b], dens_sem.at[b], column_device(b))
    lab_rx[pl.ds(0, cap), :] = lab_acc[pl.ds(0, cap), :]
    dens = jnp.where(block_lanes(0), dens_row, 0.0)
    for b in range(1, G):
        arrive(dens_rx.at[b], dens_sem.at[b])
        dens = dens + jnp.where(block_lanes(b), dens_rx[b], 0.0)
    hit = poscol[...] == lane
    weight_ref[...] = row_of(1.0 / jnp.sum(jnp.where(hit, dens, 0.0), axis=1, keepdims=True))
    for b in range(1, G):
        arrive(lab_rx.at[pl.ds(b * cap, cap)], lab_sem.at[b])
    pick = hit.astype(jnp.float32).astype(jnp.bfloat16)
    rest = lab_rx[...]
    total = jnp.zeros((rows, LABELS), jnp.float32)
    for _ in range(3):
        piece = rest.astype(jnp.bfloat16)
        total = total + jnp.dot(pick, piece, preferred_element_type=jnp.float32)
        rest = rest - piece.astype(jnp.float32)
    label_ref[...] = total
    for copy in sent:
        copy.wait_send()


def on_device(mesh_shape, embeddings, centroids, cluster, labels):
    rows, width = embeddings.shape
    plan = Plan(mesh_shape, rows, width, centroids.shape[0])
    G, places = plan.groups, plan.places
    near, far = plan.xs - 1 + plan.sub - 1, (plan.xs - 1) * (plan.sub - 1)
    copies = 4 * (G - 1) + places - 1 + G * (near + 1 + near + far + far)
    vmem = pl.BlockSpec(memory_space=pltpu.VMEM)
    weight, label_sums = pl.pallas_call(
        functools.partial(kernel, plan),
        out_shape=(
            jax.ShapeDtypeStruct((1, rows), jnp.float32),
            jax.ShapeDtypeStruct((rows, LABELS), jnp.float32),
        ),
        in_specs=[vmem] * 5,
        out_specs=(vmem, vmem),
        scratch_shapes=[
            pltpu.VMEM((plan.slots, width), jnp.bfloat16),
            pltpu.VMEM((places, plan.slots, width), jnp.bfloat16),
            pltpu.VMEM((places, 1, plan.slots), jnp.int32),
            pltpu.VMEM((1, plan.slots), jnp.int32),
            pltpu.VMEM((G, 1, plan.slots), jnp.int32),
            pltpu.VMEM((plan.slots, 1), jnp.int32),
            pltpu.VMEM((rows, 1), jnp.int32),
            pltpu.VMEM((plan.slots, 128), jnp.float32),
            pltpu.VMEM((plan.slots, LABELS), jnp.float32),
            pltpu.VMEM((1, plan.slots), jnp.float32),
            pltpu.VMEM((G, 1, plan.slots), jnp.float32),
            pltpu.VMEM((plan.slots, LABELS), jnp.float32),
            pltpu.SemaphoreType.DMA((copies,)),
            pltpu.SemaphoreType.DMA((places, G)),
            pltpu.SemaphoreType.DMA((G,)),
            pltpu.SemaphoreType.DMA((places,)),
            pltpu.SemaphoreType.DMA((G,)),
            pltpu.SemaphoreType.DMA((G,)),
        ],
        compiler_params=pltpu.CompilerParams(
            collective_id=0, has_side_effects=True, vmem_limit_bytes=48 * 1024 * 1024
        ),
    )(
        embeddings,
        centroids,
        cluster.reshape(rows, 1),
        cluster.reshape(1, rows),
        labels.reshape(rows, 1),
    )
    return (weight.reshape(rows), label_sums)


def solution(mesh):
    in_specs = (P(("ingest", "pair"), None), P(), P(("ingest", "pair")), P(("ingest", "pair")))
    out_specs = (P(("ingest", "pair")), P(("ingest", "pair"), None))
    return jax.shard_map(
        functools.partial(on_device, dict(mesh.shape)),
        mesh=mesh,
        in_specs=in_specs,
        out_specs=out_specs,
        check_vma=False,
    )
```

time: 196 us -> 92.1 us (0.47)
  Pallas kernels: 0 us -> 86.8 us
  blocking collectives: 72.5 us -> 0 us
  waiting for transfers between devices: 66.8 us -> 0 us
  matrix products: 31.3 us -> 0 us
  starting transfers between devices: 7.78 us -> 0 us
  other arithmetic: 8.08 us -> 0.6 us
  local copies, waits for them, and re-layouts: 8.23 us -> 3.84 us
    pallas_call x0 -> x1, Pallas kernels: none -> 86.8 us  [on_device(): pl.pallas_call(functools.partial(kernel, plan), out_shape=(jax.ShapeDtype...]
    all_to_all x2 -> x0, blocking collectives: 72.5 us -> none  [the longest x1 62.9 us: on_device(): lax.all_to_all(send_rows, ('ingest', 'pair'), split_axis=0, concat_axis=0...]
    all_to_all x2 -> x0, waiting for transfers between devices: 64.5 us -> none  [the longest x1 47 us: on_device(): lax.all_to_all(send_meta, ('ingest', 'pair'), split_axis=0, concat_axis=0...]
    dot_general x13 -> x0, matrix products: 31.3 us -> none  [the longest x6 22.6 us: kernel_block(): lax.dot_general(queries, key_rows, (((1,), (1,)), ((), ())), preferred_el...]
    all_to_all x2 -> x0, starting transfers between devices: 5.43 us -> none  [the longest x1 2.81 us: on_device(): lax.all_to_all(send_meta, ('ingest', 'pair'), split_axis=0, concat_axis=0...]
    gather x2 -> x0, local copies, waits for them, and re-layouts: 4.15 us -> none  [on_device(): return (1.0 / home_density[slot_index], home_labels[slot_index])]
    scatter x1 -> x0, other arithmetic: 3.65 us -> none  [pack_rows(): jnp.zeros((total_slots, unit.shape[1]), jnp.bfloat16).at[slot_index]]
    unnamed x6 -> x9, local copies, waits for them, and re-layouts: 0.02 us -> 2.94 us
  transfers between devices with their start and end apart: 4 -> 0, of which waited for: 3 -> 0; matrix products, arithmetic and copies ran while one was open for 4% -> 0% of each run, Pallas kernels for 0% -> 0%
where the time goes in v1:
time: 92.1 us; the launch traced here: 91.9 us
  Pallas kernels  86.8 us (94%)
  local copies, waits for them, and re-layouts  3.84 us (4%)
    pallas_call x1, Pallas kernels, on_device(): pl.pallas_call(functools.partial(kernel, plan), out_shape=(jax.ShapeDtype...  86.8 us
    unnamed x9, local copies, waits for them, and re-layouts  2.94 us

profile of v1, /device:TPU:0, one launch (start us, length us, event | category | flops | bytes accessed | tf_op | source)
XLA Modules:
  0.0 91.9 jit_solution(11031050863136115241)
XLA Ops:
  0.6 0.0 copy-start.3
  0.6 0.7 reshape.17.crow_ref
  1.3 0.0 copy-done.3
  1.3 0.0 copy-start.2
  1.3 0.1 reshape.21.lcol_ref
  1.4 0.6 copy-done.2
  2.0 0.0 copy-start.1
  2.0 0.1 reshape.20.ccol_ref
  2.1 0.6 copy-done.1
  2.8 0.0 copy-start
  2.8 1.1 %copy-done = bf16[384,768]{1,0:T(8,128)(2,1)S(1)} copy-done((bf16[384,768]{1,0:T(8,128)(2,1)S(1)}, bf16[384,768]{1,0:T(8,128)(2,1)}, u32[]{:S(2)}) %copy-start) | copy-done | bytes 589848
  3.8 86.8 %shard_map.59 = (f32[1,384]{1,0:T(1,128)S(1)}, f32[384,128]{1,0:T(8,128)S(1)}) custom-call(bf16[384,768]{1,0:T(8,128)(2,1)S(1)} %copy-done, bf16[16,768]{1,0:T(8,128)(2,1)S(1)} %copy-done.1, s32[384,1]{1,0:T(8,128)S(1)} %reshape.20.ccol_ref, s32[1,384]{1,0:T(1,128)S(1)} %reshape.17.crow_ref, s32[384,1]{1,0:T(8,128)S(1)} %reshape.21.lcol_ref), custom_call_target="tpu_custom_call" | custom-call | tf_op jit(solution)/shard_map/pallas_call | solution.py:356
  90.6 0.6 reduce
  91.2 0.7 copy.9
Async XLA Ops:
  0.6 0.7 copy-start.3
  1.3 0.7 copy-start.2
  2.0 0.7 copy-start.1
  2.8 1.1 %copy-start = (bf16[384,768]{1,0:T(8,128)(2,1)S(1)}, bf16[384,768]{1,0:T(8,128)(2,1)}, u32[]{:S(2)}) copy-start(bf16[384,768]{1,0:T(8,128)(2,1)} %emb_ref.1) | copy-start | bytes 1769476

commit v2 on v1

--- a/solution.py
+++ b/solution.py
@@ -26,6 +26,7 @@
         self.cap = 2 * rows // self.groups
         self.slots = self.groups * self.cap
         self.places = self.xs * self.sub * CORES
+        self.order = sorted(range(self.groups), key=lambda o: (min(o, self.groups - o), o))
         self.chunk = 256 if self.slots % 256 == 0 else 128
 
     def place(self, dx, dy, dc):
@@ -76,11 +77,10 @@
     plan,
     emb_ref,
     cent_ref,
-    ccol_ref,
-    crow_ref,
-    lcol_ref,
+    code_ref,
     weight_ref,
     label_ref,
+    emb,
     packed,
     keys,
     codes,
@@ -99,8 +99,9 @@
     code_sem,
     dens_sem,
     lab_sem,
+    emb_sem,
 ):
-    G, cap, slots, sub = plan.groups, plan.cap, plan.slots, plan.sub
+    G, cap, slots, sub, order = plan.groups, plan.cap, plan.slots, plan.sub, plan.order
     ingest = lax.axis_index("ingest")
     pair = lax.axis_index("pair")
     x, core = ingest // CORES, ingest % CORES
@@ -115,6 +116,8 @@
     def column_device(dz):
         return (ingest, lax.rem(z + dz, G) * sub + y)
 
+    fetch = pltpu.make_async_copy(emb_ref, emb, emb_sem)
+    fetch.start()
     barrier = pltpu.get_barrier_semaphore()
     for dz in range(1, G):
         pl.semaphore_signal(barrier, inc=1, device_id=column_device(dz), device_id_type=MESH)
@@ -122,12 +125,17 @@
         pl.semaphore_signal(barrier, inc=1, device_id=plane_device(*offset), device_id_type=MESH)
 
     def slot_of(cluster, rank):
-        block = z - group_of(plan, cluster)
-        block = jnp.where(block < 0, block + G, block)
+        offset = z - group_of(plan, cluster)
+        offset = jnp.where(offset < 0, offset + G, offset)
+        block = jnp.zeros(offset.shape, jnp.int32)
+        for b in range(1, G):
+            block = jnp.where(offset == order[b], b, block)
         return block * cap + rank
 
     rows = plan.rows
-    ccol, crow = ccol_ref[...], crow_ref[...]
+    code_row = code_ref[...]
+    code_col = column_of(code_row)
+    crow, ccol = code_row >> 7, code_col >> 7
     same = group_of(plan, ccol) == group_of(plan, crow)
     first = lax.broadcasted_iota(jnp.int32, (rows, rows), 0)
     second = lax.broadcasted_iota(jnp.int32, (rows, rows), 1)
@@ -136,15 +144,15 @@
     pos_row = slot_of(crow, rank_row)
     pos_col = slot_of(ccol, rank_col)
     poscol[...] = pos_col
-    code_col = ccol * LABELS + lcol_ref[...] + 1
     lane = lax.broadcasted_iota(jnp.int32, (rows, slots), 1)
-    code_tx[...] = jnp.sum(jnp.where(pos_col == lane, code_col, 0), axis=0, keepdims=True)
+    code_tx[...] = jnp.sum(jnp.where(pos_col == lane, code_col + 1, 0), axis=0, keepdims=True)
 
     lookup = (ccol == lax.broadcasted_iota(jnp.int32, (rows, plan.clusters), 1)).astype(
         jnp.float32
     ).astype(jnp.bfloat16)
     centre = jnp.dot(lookup, cent_ref[...], preferred_element_type=jnp.float32)
-    shifted = centre + emb_ref[...].astype(jnp.float32)
+    fetch.wait()
+    shifted = centre + emb[...].astype(jnp.float32)
     scale = lax.rsqrt(jnp.sum(shifted * shifted, axis=1, keepdims=True) + EPSILON)
     unit = (shifted * scale).astype(jnp.bfloat16)
     for b in range(G):
@@ -159,7 +167,7 @@
 
     pl.semaphore_wait(barrier, G - 1 + plan.places - 1)
 
-    sent = []
+    sent, dispatched = [], []
 
     def send(src, dst, sem, device):
         copy = pltpu.make_async_remote_copy(
@@ -183,14 +191,20 @@
             device_id_type=MESH,
         ).wait_recv()
 
-    def part(place, b):
-        return keys.at[place, pl.ds(b * cap, cap)]
-
-    def pass_on(src_place, to_place, b, device):
-        send(part(src_place, b), part(to_place, b), row_sem.at[to_place, b], device)
+    def part(place, b, half=None):
+        if half is None:
+            return keys.at[place, pl.ds(b * cap, cap)]
+        return keys.at[place, pl.ds(b * cap + half * (cap // 2), cap // 2)]
+
+    def pass_on(src_place, to_place, b, device, half=None):
+        send(part(src_place, b, half), part(to_place, b, half), row_sem.at[to_place, b], device)
+
+    here = {(0, 0)}
 
     def rows_arrive(place, b):
-        arrive(part(place, b), row_sem.at[place, b])
+        if (place, b) not in here:
+            here.add((place, b))
+            arrive(part(place, b), row_sem.at[place, b])
 
     xrange, yrange = range(1, plan.xs), range(1, sub)
 
@@ -204,19 +218,17 @@
     def forward_near(b):
         for dx in xrange:
             rows_arrive(plan.place(dx, 0, 0), b)
-            if b % 2 == 0:
-                for dy in yrange:
-                    pass_on(
-                        plan.place(dx, 0, 0), plan.place(dx, -dy, 0), b, plane_device(0, dy, 0)
-                    )
+            for dy in yrange:
+                pass_on(
+                    plan.place(dx, 0, 0), plan.place(dx, -dy, 0), b, plane_device(0, dy, 0), 0
+                )
             pass_on(plan.place(dx, 0, 0), plan.place(dx, 0, 1), b, plane_device(0, 0, 1))
         for dy in yrange:
             rows_arrive(plan.place(0, dy, 0), b)
-            if b % 2 == 1:
-                for dx in xrange:
-                    pass_on(
-                        plan.place(0, dy, 0), plan.place(-dx, dy, 0), b, plane_device(dx, 0, 0)
-                    )
+            for dx in xrange:
+                pass_on(
+                    plan.place(0, dy, 0), plan.place(-dx, dy, 0), b, plane_device(dx, 0, 0), 1
+                )
             pass_on(plan.place(0, dy, 0), plan.place(0, dy, 1), b, plane_device(0, 0, 1))
 
     def forward_far(b):
@@ -225,12 +237,19 @@
                 rows_arrive(plan.place(dx, dy, 0), b)
                 pass_on(plan.place(dx, dy, 0), plan.place(dx, dy, 1), b, plane_device(0, 0, 1))
 
-    for b in range(1, G):
-        send(code_tx, code_rx.at[b], code_rx_sem.at[b], column_device(G - b))
-    for b in range(1, G):
+    def dispatch(b):
         send(
-            packed.at[pl.ds(b * cap, cap)], part(0, b), row_sem.at[0, b], column_device(G - b)
-        )
+            packed.at[pl.ds(b * cap, cap)],
+            part(0, b),
+            row_sem.at[0, b],
+            column_device(G - order[b]),
+        )
+        dispatched.append(sent[-1])
+        return sent[-1]
+
+    for b in range(1, G):
+        send(code_tx, code_rx.at[b], code_rx_sem.at[b], column_device(G - order[b]))
+    going = dispatch(1)
     spread(0)
 
     lane_row = lax.broadcasted_iota(jnp.int32, (1, slots), 1)
@@ -255,7 +274,10 @@
     chunk = plan.chunk
     steps = slots // chunk
 
-    def compute(place):
+    def compute(place, first_step, last_step):
+        for b in range((last_step * chunk - 1) // cap + 1):
+            rows_arrive(place, b)
+
         def body(step, carry):
             start = pl.multiple_of(step * chunk, chunk)
             key_rows = keys[place, pl.ds(start, chunk), :]
@@ -283,48 +305,47 @@
             )
             return carry
 
-        lax.fori_loop(0, steps, body, 0)
-
-    for b in range(1, G):
+        lax.fori_loop(first_step, last_step, body, 0)
+
+    for b in range(1, G):
+        going.wait_send()
+        if b + 1 < G:
+            going = dispatch(b + 1)
         rows_arrive(0, b)
         spread(b)
         forward_near(b - 1)
         if b >= 2:
             forward_far(b - 2)
 
-    def arrived(place):
-        for b in range(G):
-            rows_arrive(place, b)
-
+    near = [(dx, 0) for dx in xrange] + [(0, dy) for dy in yrange]
+    far = [(dx, dy) for dx in xrange for dy in yrange]
+    compute(0, 0, steps)
+    compute(plan.place(0, 0, 1), 0, steps)
+    for dx, dy in near:
+        compute(plan.place(dx, dy, 0), 0, steps - 1)
+    forward_near(G - 1)
     forward_far(G - 2)
-    compute(0)
-    forward_near(G - 1)
-    arrived(plan.place(0, 0, 1))
-    compute(plan.place(0, 0, 1))
-    near = [(dx, 0) for dx in xrange] + [(0, dy) for dy in yrange]
     for dx, dy in near:
-        compute(plan.place(dx, dy, 0))
+        compute(plan.place(dx, dy, 1), 0, steps - 1)
+    for dc in range(CORES):
+        for dx, dy in far:
+            compute(plan.place(dx, dy, dc), 0, steps - 1)
     forward_far(G - 1)
-    for dx, dy in near:
-        arrived(plan.place(dx, dy, 1))
-        compute(plan.place(dx, dy, 1))
-    for dx in xrange:
-        for dy in yrange:
-            compute(plan.place(dx, dy, 0))
-            arrived(plan.place(dx, dy, 1))
-            compute(plan.place(dx, dy, 1))
-
+    for dx, dy in near + far:
+        for dc in range(CORES):
+            compute(plan.place(dx, dy, dc), steps - 1, steps)
+
+    dens_row = row_of(jnp.sum(dens_acc[...], axis=1, keepdims=True))
+    dens_tx[...] = dens_row
+    for b in range(1, G):
+        send(dens_tx, dens_rx.at[b], dens_sem.at[b], column_device(order[b]))
     for b in range(1, G):
         send(
             lab_acc.at[pl.ds(b * cap, cap)],
             lab_rx.at[pl.ds(b * cap, cap)],
             lab_sem.at[b],
-            column_device(b),
-        )
-    dens_row = row_of(jnp.sum(dens_acc[...], axis=1, keepdims=True))
-    dens_tx[...] = dens_row
-    for b in range(1, G):
-        send(dens_tx, dens_rx.at[b], dens_sem.at[b], column_device(b))
+            column_device(order[b]),
+        )
     lab_rx[pl.ds(0, cap), :] = lab_acc[pl.ds(0, cap), :]
     dens = jnp.where(block_lanes(0), dens_row, 0.0)
     for b in range(1, G):
@@ -343,7 +364,8 @@
         rest = rest - piece.astype(jnp.float32)
     label_ref[...] = total
     for copy in sent:
-        copy.wait_send()
+        if not any(copy is other for other in dispatched):
+            copy.wait_send()
 
 
 def on_device(mesh_shape, embeddings, centroids, cluster, labels):
@@ -351,7 +373,7 @@
     plan = Plan(mesh_shape, rows, width, centroids.shape[0])
     G, places = plan.groups, plan.places
     near, far = plan.xs - 1 + plan.sub - 1, (plan.xs - 1) * (plan.sub - 1)
-    copies = 4 * (G - 1) + places - 1 + G * (near + 1 + near + far + far)
+    copies = 4 * (G - 1) + places - 1 + G * (near + 1 + near + 2 * far + far)
     vmem = pl.BlockSpec(memory_space=pltpu.VMEM)
     weight, label_sums = pl.pallas_call(
         functools.partial(kernel, plan),
@@ -359,9 +381,10 @@
             jax.ShapeDtypeStruct((1, rows), jnp.float32),
             jax.ShapeDtypeStruct((rows, LABELS), jnp.float32),
         ),
-        in_specs=[vmem] * 5,
+        in_specs=[pl.BlockSpec(memory_space=pl.ANY), vmem, vmem],
         out_specs=(vmem, vmem),
         scratch_shapes=[
+            pltpu.VMEM((rows, width), jnp.bfloat16),
             pltpu.VMEM((plan.slots, width), jnp.bfloat16),
             pltpu.VMEM((places, plan.slots, width), jnp.bfloat16),
             pltpu.VMEM((places, 1, plan.slots), jnp.int32),
@@ -380,6 +403,7 @@
             pltpu.SemaphoreType.DMA((places,)),
             pltpu.SemaphoreType.DMA((G,)),
             pltpu.SemaphoreType.DMA((G,)),
+            pltpu.SemaphoreType.DMA,
         ],
         compiler_params=pltpu.CompilerParams(
             collective_id=0, has_side_effects=True, vmem_limit_bytes=48 * 1024 * 1024
@@ -387,9 +411,7 @@
     )(
         embeddings,
         centroids,
-        cluster.reshape(rows, 1),
-        cluster.reshape(1, rows),
-        labels.reshape(rows, 1),
+        (cluster * LABELS + labels).reshape(1, rows),
     )
     return (weight.reshape(rows), label_sums)
 

time: 92.1 us -> 72.9 us (0.79)
  Pallas kernels: 86.8 us -> 68.2 us
  local copies, waits for them, and re-layouts: 3.84 us -> 2.48 us
    pallas_call x1, Pallas kernels: 86.8 us -> 68.2 us  [on_device(): pl.pallas_call(functools.partial(kernel, plan), out_shape=(jax.ShapeDtype...]
    unnamed x9 -> x5, local copies, waits for them, and re-layouts: 2.94 us -> 2.48 us
where the time goes in v2:
time: 72.9 us; the launch traced here: 72.7 us
  Pallas kernels  68.2 us (94%)
  local copies, waits for them, and re-layouts  2.48 us (3%)
  other arithmetic  1.3 us (2%)
    pallas_call x1, Pallas kernels, on_device(): pl.pallas_call(functools.partial(kernel, plan), out_shape=(jax.ShapeDtype...  68.2 us
    unnamed x5, local copies, waits for them, and re-layouts  2.48 us

profile of v2, /device:TPU:0, one launch (start us, length us, event | category | flops | bytes accessed | tf_op | source)
XLA Modules:
  0.0 72.7 jit_solution(2879933172207396902)
XLA Ops:
  0.6 0.7 multiply_add_fusion
  1.3 0.0 copy-start
  1.3 1.1 %copy-done = bf16[384,768]{1,0:T(8,128)(2,1)S(1)} copy-done((bf16[384,768]{1,0:T(8,128)(2,1)S(1)}, bf16[384,768]{1,0:T(8,128)(2,1)}, u32[]{:S(2)}) %copy-start) | copy-done | bytes 589848
  2.4 0.0 copy-start.1
  2.4 0.7 %copy-done.1 = bf16[16,768]{1,0:T(8,128)(2,1)S(1)} copy-done((bf16[16,768]{1,0:T(8,128)(2,1)S(1)}, bf16[16,768]{1,0:T(8,128)(2,1)}, u32[]{:S(2)}) %copy-start.1) | copy-done | bytes 24600
  3.1 68.2 %shard_map.59 = (f32[1,384]{1,0:T(1,128)S(1)}, f32[384,128]{1,0:T(8,128)S(1)}) custom-call(bf16[384,768]{1,0:T(8,128)(2,1)S(1)} %copy-done, bf16[16,768]{1,0:T(8,128)(2,1)S(1)} %copy-done.1, s32[1,384]{1,0:T(1,128)S(1)} %reshape.10.code_ref), custom_call_target="tpu_custom_call" | custom-call | tf_op jit(solution)/shard_map/pallas_call | solution.py:378
  71.4 0.6 reduce
  72.0 0.7 copy.7
  (1 shorter events, 0.0 us)
Async XLA Ops:
  1.3 1.1 %copy-start = (bf16[384,768]{1,0:T(8,128)(2,1)S(1)}, bf16[384,768]{1,0:T(8,128)(2,1)}, u32[]{:S(2)}) copy-start(bf16[384,768]{1,0:T(8,128)(2,1)} %emb_ref.1) | copy-start | bytes 1769476
  2.4 0.7 %copy-start.1 = (bf16[16,768]{1,0:T(8,128)(2,1)S(1)}, bf16[16,768]{1,0:T(8,128)(2,1)}, u32[]{:S(2)}) copy-start(bf16[16,768]{1,0:T(8,128)(2,1)} %cent_ref.1) | copy-start | bytes 73732

commit v3 on v2

--- a/solution.py
+++ b/solution.py
@@ -8,6 +8,7 @@
 from jax.sharding import PartitionSpec as P
 
 LABELS = 128
+LEVELS = 32766.0
 SHARPNESS = 8.0
 EPSILON = 1e-06
 CORES = 2
@@ -92,6 +93,7 @@
     lab_acc,
     dens_tx,
     dens_rx,
+    lab_tx,
     lab_rx,
     send_sem,
     row_sem,
@@ -305,7 +307,7 @@
             )
             return carry
 
-        lax.fori_loop(first_step, last_step, body, 0)
+        lax.fori_loop(first_step, last_step, body, 0, unroll=True)
 
     for b in range(1, G):
         going.wait_send()
@@ -330,39 +332,50 @@
     for dc in range(CORES):
         for dx, dy in far:
             compute(plan.place(dx, dy, dc), 0, steps - 1)
+    for dx, dy in near:
+        compute(plan.place(dx, dy, 0), steps - 1, steps)
     forward_far(G - 1)
-    for dx, dy in near + far:
-        for dc in range(CORES):
+    for dx, dy in near:
+        compute(plan.place(dx, dy, 1), steps - 1, steps)
+    for dc in range(CORES):
+        for dx, dy in far:
             compute(plan.place(dx, dy, dc), steps - 1, steps)
 
+    largest = jnp.maximum(jnp.max(lab_acc[...], axis=1, keepdims=True), 1e-30)
     dens_row = row_of(jnp.sum(dens_acc[...], axis=1, keepdims=True))
-    dens_tx[...] = dens_row
+    largest_row = row_of(largest)
+    dens_tx[:, :slots] = dens_row
+    dens_tx[:, slots:] = largest_row
+    lab_tx[...] = (lab_acc[...] * (LEVELS / largest) + 0.5).astype(jnp.int32).astype(jnp.int16)
     for b in range(1, G):
         send(dens_tx, dens_rx.at[b], dens_sem.at[b], column_device(order[b]))
     for b in range(1, G):
         send(
-            lab_acc.at[pl.ds(b * cap, cap)],
+            lab_tx.at[pl.ds(b * cap, cap)],
             lab_rx.at[pl.ds(b * cap, cap)],
             lab_sem.at[b],
             column_device(order[b]),
         )
-    lab_rx[pl.ds(0, cap), :] = lab_acc[pl.ds(0, cap), :]
+    lab_rx[pl.ds(0, cap), :] = lab_tx[pl.ds(0, cap), :]
     dens = jnp.where(block_lanes(0), dens_row, 0.0)
+    unit_row = jnp.where(block_lanes(0), largest_row, 0.0)
     for b in range(1, G):
         arrive(dens_rx.at[b], dens_sem.at[b])
-        dens = dens + jnp.where(block_lanes(b), dens_rx[b], 0.0)
+        dens = dens + jnp.where(block_lanes(b), dens_rx[b, :, :slots], 0.0)
+        unit_row = unit_row + jnp.where(block_lanes(b), dens_rx[b, :, slots:], 0.0)
     hit = poscol[...] == lane
     weight_ref[...] = row_of(1.0 / jnp.sum(jnp.where(hit, dens, 0.0), axis=1, keepdims=True))
+    unit_col = jnp.sum(jnp.where(hit, unit_row, 0.0), axis=1, keepdims=True) / LEVELS
     for b in range(1, G):
         arrive(lab_rx.at[pl.ds(b * cap, cap)], lab_sem.at[b])
     pick = hit.astype(jnp.float32).astype(jnp.bfloat16)
-    rest = lab_rx[...]
+    rest = lab_rx[...].astype(jnp.int32).astype(jnp.float32)
     total = jnp.zeros((rows, LABELS), jnp.float32)
-    for _ in range(3):
+    for _ in range(2):
         piece = rest.astype(jnp.bfloat16)
         total = total + jnp.dot(pick, piece, preferred_element_type=jnp.float32)
         rest = rest - piece.astype(jnp.float32)
-    label_ref[...] = total
+    label_ref[...] = total * unit_col
     for copy in sent:
         if not any(copy is other for other in dispatched):
             copy.wait_send()
@@ -394,9 +407,10 @@
             pltpu.VMEM((rows, 1), jnp.int32),
             pltpu.VMEM((plan.slots, 128), jnp.float32),
             pltpu.VMEM((plan.slots, LABELS), jnp.float32),
-            pltpu.VMEM((1, plan.slots), jnp.float32),
-            pltpu.VMEM((G, 1, plan.slots), jnp.float32),
-            pltpu.VMEM((plan.slots, LABELS), jnp.float32),
+            pltpu.VMEM((1, 2 * plan.slots), jnp.float32),
+            pltpu.VMEM((G, 1, 2 * plan.slots), jnp.float32),
+            pltpu.VMEM((plan.slots, LABELS), jnp.int16),
+            pltpu.VMEM((plan.slots, LABELS), jnp.int16),
             pltpu.SemaphoreType.DMA((copies,)),
             pltpu.SemaphoreType.DMA((places, G)),
             pltpu.SemaphoreType.DMA((G,)),

time: 72.9 us -> 68 us (0.933)
  Pallas kernels: 68.2 us -> 63.3 us
    pallas_call x1, Pallas kernels: 68.2 us -> 63.3 us  [on_device(): pl.pallas_call(functools.partial(kernel, plan), out_shape=(jax.ShapeDtype...]
where the time goes in v3:
time: 68 us; the launch traced here: 67.7 us
  Pallas kernels  63.3 us (93%)
  local copies, waits for them, and re-layouts  2.48 us (4%)
  other arithmetic  1.3 us (2%)
    pallas_call x1, Pallas kernels, on_device(): pl.pallas_call(functools.partial(kernel, plan), out_shape=(jax.ShapeDtype...  63.3 us
    unnamed x5, local copies, waits for them, and re-layouts  2.48 us

profile of v3, /device:TPU:0, one launch (start us, length us, event | category | flops | bytes accessed | tf_op | source)
XLA Modules:
  0.0 67.7 jit_solution(14559879484994595893)
XLA Ops:
  0.6 0.7 %multiply_add_fusion = s32[384]{0:T(512)S(1)} fusion(s32[384]{0:T(512)} %param.7, s32[384]{0:T(512)} %param.6), kind=kLoop, calls=%fused_computation | loop fusion | flops 768 | bytes 4608 | tf_op jit(solution)/shard_map/add | solution.py:428
  1.3 0.0 copy-start
  1.3 1.1 %copy-done = bf16[384,768]{1,0:T(8,128)(2,1)S(1)} copy-done((bf16[384,768]{1,0:T(8,128)(2,1)S(1)}, bf16[384,768]{1,0:T(8,128)(2,1)}, u32[]{:S(2)}) %copy-start) | copy-done | bytes 589848
  2.4 0.0 copy-start.1
  2.4 0.7 %copy-done.1 = bf16[16,768]{1,0:T(8,128)(2,1)S(1)} copy-done((bf16[16,768]{1,0:T(8,128)(2,1)S(1)}, bf16[16,768]{1,0:T(8,128)(2,1)}, u32[]{:S(2)}) %copy-start.1) | copy-done | bytes 24600
  3.1 63.3 %shard_map.59 = (f32[1,384]{1,0:T(1,128)S(1)}, f32[384,128]{1,0:T(8,128)S(1)}) custom-call(bf16[384,768]{1,0:T(8,128)(2,1)S(1)} %copy-done, bf16[16,768]{1,0:T(8,128)(2,1)S(1)} %copy-done.1, s32[1,384]{1,0:T(1,128)S(1)} %reshape.10.code_ref), custom_call_target="tpu_custom_call" | custom-call | tf_op jit(solution)/shard_map/pallas_call | solution.py:391
  66.5 0.6 reduce
  67.1 0.7 copy.7
  (1 shorter events, 0.0 us)
Async XLA Ops:
  1.3 1.1 %copy-start = (bf16[384,768]{1,0:T(8,128)(2,1)S(1)}, bf16[384,768]{1,0:T(8,128)(2,1)}, u32[]{:S(2)}) copy-start(bf16[384,768]{1,0:T(8,128)(2,1)} %emb_ref.1) | copy-start | bytes 1769476
  2.4 0.7 %copy-start.1 = (bf16[16,768]{1,0:T(8,128)(2,1)S(1)}, bf16[16,768]{1,0:T(8,128)(2,1)}, u32[]{:S(2)}) copy-start(bf16[16,768]{1,0:T(8,128)(2,1)} %cent_ref.1) | copy-start | bytes 73732
